TPU v7x, 32 devices: a whole 2x2x4 slice. The times are simulated.
32 devices in a mesh: space: 8 (over z, core), member: 4 (over y, x).
Axes of the slice: x: 2, y: 2, z: 4, core: 2. Of those that a mesh axis runs over, the one named last changes fastest.
Arguments:
- perturbation: float32 [4, 4, 16, 16, 1024], P('member', None, None, None, 'space'), may hold values from -6 to 6
- trajectory: bfloat16 [3, 16, 6, 16, 1024], P(None, 'member', None, None, 'space'), may hold values from -0.5 to 0.5
- site_col: int32 [8, 8, 128], P(None, 'space'), may hold values from 0 to 2047
- site_lev: int32 [8, 8, 128], P(None, 'space'), may hold values from 0 to 15
- obs_counts: int32 [8, 8], P(None, 'space'), may hold values from 0 to 128, as said below
- obs_weights: float32 [8, 8, 4, 128], P('space'), may hold values from -3 to 3
Outputs:
- final_state: float32 [4, 4, 16, 16, 1024], P('member', None, None, None, 'space')
- obs_equiv: float32 [4, 8, 8, 128], P('member', 'space')
Inputs may be any that keep to these rules, and one draw needn't show every extreme that they name: obs_counts[o, s] is the number of live leading slots of owner o in tile s; some pair has exactly 128, and owners differ in load by up to four times.
All inputs are finite; a program needn't handle non-finite values.
Results may differ from a plain program's by a relative error of at most 0.0003.
Values may be sent and summed in bfloat16 or wider, within the bound.
A program may use at most 64 MiB of HBM per device.

v0:
```python
import jax
import jax.numpy as jnp
from jax import lax
from jax.sharding import PartitionSpec as P


def with_halo(array, sides, width):
    for axis, dim in sides:
        size, length = (lax.axis_size(axis), array.shape[dim])
        up = [(i, (i + 1) % size) for i in range(size)]
        down = [(j, i) for i, j in up]
        last = lax.slice_in_dim(array, length - width, length, axis=dim)
        first = lax.slice_in_dim(array, 0, width, axis=dim)
        before = lax.ppermute(last, axis, up)
        after = lax.ppermute(first, axis, down)
        array = jnp.concatenate([before, array, after], axis=dim)
    return array


def update(state, east, west, coef):
    rows = jnp.pad(state, ((0, 0), (0, 0), (0, 0), (1, 1), (0, 0)))
    north = rows[:, :, :, 2:, :]
    south = rows[:, :, :, :-2, :]
    planes = coef.astype(jnp.float32)
    along = planes[:, 0][None, None]
    across = planes[:, 1][None, None]
    fresh = state - along * (east - west) * 0.5 + 0.5 * along * along * (east - 2.0 * state + west)
    fresh = (
        fresh
        - across * (north - south) * 0.5
        + 0.5 * across * across * (north - 2.0 * state + south)
    )
    wind_u = state[:, 0]
    wind_v = state[:, 1]
    temper = fresh[:, 2] - (planes[:, 2][None] * wind_u + planes[:, 3][None] * wind_v)
    humid = fresh[:, 3] - (planes[:, 4][None] * wind_u + planes[:, 5][None] * wind_v)
    return jnp.stack([fresh[:, 0], fresh[:, 1], temper, humid], axis=1)


def advance(state, coef):
    padded = with_halo(state, (("space", 4),), 1)
    return update(state, padded[..., 2:], padded[..., :-2], coef)


def run_steps(state, get_planes, nsteps):
    for step in range(nsteps):
        state = advance(state, get_planes(step))
    return state


def on_device(perturbation, trajectory, site_col, site_lev, obs_counts, obs_weights):
    state = perturbation
    nsteps = trajectory.shape[0]
    gathered = lax.all_gather(trajectory, "member", axis=1, tiled=True)
    state = run_steps(state, lambda step: gathered[step], nsteps)
    levels = state.shape[2]
    lat_rows = state.shape[3]
    lon_cols = state.shape[4]
    flat = state.reshape(4, levels * lat_rows * lon_cols)
    index = site_lev[:, 0, :] * (lat_rows * lon_cols) + site_col[:, 0, :]
    tiles = index.shape[0]
    slots = index.shape[1]
    picked = jnp.take(flat, index.reshape(-1), axis=1).reshape(4, tiles, slots)
    picked = jnp.transpose(picked, (1, 0, 2))
    live = jnp.arange(slots, dtype=jnp.int32)[None, :] < obs_counts[:, 0][:, None]
    outgoing = jnp.where(live[:, None, :], picked, jnp.float32(0.0))
    received = lax.all_to_all(outgoing, "space", split_axis=0, concat_axis=0, tiled=True)
    summed = jnp.sum(obs_weights[0] * received, axis=1)
    obs_equiv = summed.reshape(1, 1, tiles, slots)
    return (state, obs_equiv)


def solution(mesh):
    in_specs = (
        P("member", None, None, None, "space"),
        P(None, "member", None, None, "space"),
        P(None, "space", None),
        P(None, "space", None),
        P(None, "space"),
        P("space", None, None, None),
    )
    out_specs = (P("member", None, None, None, "space"), P("member", "space", None, None))
    return jax.shard_map(
        on_device, mesh=mesh, in_specs=in_specs, out_specs=out_specs, check_vma=False
    )
```

profile of v0, /device:TPU:0, one launch (start us, length us, event | category | flops | bytes accessed | tf_op | source)
XLA Modules:
  0.0 113.1 jit_solution(4715828473758540269)
XLA Ops:
  7.2 1.7 %copy.16 = bf16[3,4,6,16,128]{4,3,1,2,0:T(8,128)(2,1)} copy(bf16[3,4,6,16,128]{4,3,2,1,0:T(8,128)(2,1)} %param.7) | data formatting | bytes 589824 | tf_op args[1]
  8.9 1.4 %fusion.30 = (f32[1,4,16,16,1]{4,3,2,1,0:T(8,128)S(1)}, f32[1,4,16,16,1]{4,3,2,1,0:T(8,128)S(1)}) fusion(f32[1,4,16,16,128]{4,3,2,1,0:T(8,128)} %param.6), kind=kLoop, calls=%fused_computation.93 | loop fusion | bytes 16384 | tf_op jit(solution)/shard_map/slice | solution.py:12
  10.4 0.5 collective-permute-start.1
  10.9 4.1 %collective-permute-start = (f32[1,4,16,16,1]{4,3,2,1,0:T(8,128)S(1)}, f32[1,4,16,16,1]{4,3,2,1,0:T(8,128)S(1)}, u32[]{:S(2)}, u32[]{:S(2)}) collective-permute-start(f32[1,4,16,16,1]{4,3,2,1,0:T(8,128)S(1)} %get-tuple-element.30), channel_id=1, source_target_pairs={{4,0},{8,4},{12,8},{16,12},{20,16},{24,20},{28,24},{0,28},{5,1},{9... | collective-permute-start | bytes 12296 | tf_op jit(solution)/shard_map/ppermute | solution.py:15
  15.0 0.7 compare_select_fusion
  15.7 0.7 iota_compare_fusion
  16.4 24.5 %all-gather.2.cloned.1.call-done = bf16[3,16,6,16,128]{4,3,1,2,0:T(8,128)(2,1)} async-done(((bf16[3,4,6,16,128]{4,3,1,2,0:T(8,128)(2,1)}), bf16[3,16,6,16,128]{4,3,1,2,0:T(8,128)(2,1)}) %all-gather.2.cloned.1.call-update) | async-done | bytes 1179664 | tf_op jit(solution)/shard_map/all_gather | solution.py:54
  40.9 1.5 %fusion.2 = (f32[16,6,16,128]{3,2,0,1:T(8,128)S(1)}, f32[16,6,16,128]{3,2,0,1:T(8,128)S(1)}, f32[16,6,16,128]{3,2,0,1:T(8,128)S(1)}) fusion(bf16[3,16,6,16,128]{4,3,1,2,0:T(8,128)(2,1)} %all-gather.2.cloned.1.call-done), kind=kLoop, calls=%fused_computation.33 | loop fusion | flops 589824 | bytes 3538944 | tf_op jit(solution)/shard_map/convert_element_type | solution.py:24
  42.4 2.7 %multiply_add_fusion.2 = f32[1,4,16,16,128]{4,3,2,1,0:T(8,128)S(1)} fusion(f32[1,4,16,16,128]{4,3,2,1,0:T(8,128)} %param.6, f32[1,4,16,16,1]{4,3,2,1,0:T(8,128)S(1)} %collective-permute-done, f32[1,4,16,16,1]{4,3,2,1,0:T(8,128)S(1)} %collective-permute-done.1, f32[16,16,128]{2,1,0:T(8,128)S(1)} %get-tuple-element.24, ...), kind=kLoop, calls=%fused_computation.27 | loop fusion | flops 2490368 | bytes 1581056 | tf_op jit(solution)/shard_map/add | solution.py:29
  45.1 1.1 fusion.25
  46.6 3.5 %collective-permute-start.2 = (f32[1,4,16,16,1]{4,3,2,1,0:T(8,128)S(1)}, f32[1,4,16,16,1]{4,3,2,1,0:T(8,128)S(1)}, u32[]{:S(2)}, u32[]{:S(2)}) collective-permute-start(f32[1,4,16,16,1]{4,3,2,1,0:T(8,128)S(1)} %get-tuple-element.28), channel_id=1, source_target_pairs={{4,0},{8,4},{12,8},{16,12},{20,16},{24,20},{28,24},{0,28},{5,1},{9... | collective-permute-start | bytes 12296 | tf_op jit(solution)/shard_map/ppermute | solution.py:15
  50.1 10.6 %collective-permute-done.3 = f32[1,4,16,16,1]{4,3,2,1,0:T(8,128)S(1)} collective-permute-done((f32[1,4,16,16,1]{4,3,2,1,0:T(8,128)S(1)}, f32[1,4,16,16,1]{4,3,2,1,0:T(8,128)S(1)}, u32[]{:S(2)}, u32[]{:S(2)}) %collective-permute-start.3) | collective-permute-done | bytes 4128 | tf_op jit(solution)/shard_map/ppermute | solution.py:14
  60.7 0.6 multiply_add_fusion.1
  61.6 1.7 %collective-permute-start.5 = (f32[1,4,16,16,1]{4,3,2,1,0:T(8,128)S(1)}, f32[1,4,16,16,1]{4,3,2,1,0:T(8,128)S(1)}, u32[]{:S(2)}, u32[]{:S(2)}) collective-permute-start(f32[1,4,16,16,1]{4,3,2,1,0:T(8,128)S(1)} %get-tuple-element.25), channel_id=1, source_target_pairs={{0,4},{4,8},{8,12},{12,16},{16,20},{20,24},{24,28},{28,0},{1,5},{5... | collective-permute-start | bytes 12296 | tf_op jit(solution)/shard_map/ppermute | solution.py:14
  63.4 1.9 %collective-permute-start.4 = (f32[1,4,16,16,1]{4,3,2,1,0:T(8,128)S(1)}, f32[1,4,16,16,1]{4,3,2,1,0:T(8,128)S(1)}, u32[]{:S(2)}, u32[]{:S(2)}) collective-permute-start(f32[1,4,16,16,1]{4,3,2,1,0:T(8,128)S(1)} %get-tuple-element.26), channel_id=1, source_target_pairs={{4,0},{8,4},{12,8},{16,12},{20,16},{24,20},{28,24},{0,28},{5,1},{9... | collective-permute-start | bytes 12296 | tf_op jit(solution)/shard_map/ppermute | solution.py:15
  65.3 12.3 %collective-permute-done.5 = f32[1,4,16,16,1]{4,3,2,1,0:T(8,128)S(1)} collective-permute-done((f32[1,4,16,16,1]{4,3,2,1,0:T(8,128)S(1)}, f32[1,4,16,16,1]{4,3,2,1,0:T(8,128)S(1)}, u32[]{:S(2)}, u32[]{:S(2)}) %collective-permute-start.5) | collective-permute-done | bytes 4128 | tf_op jit(solution)/shard_map/ppermute | solution.py:14
  77.6 0.6 multiply_add_fusion
  78.8 8.6 %copy.17 = f32[4,32768]{0,1:T(8,128)} copy(f32[4,32768]{1,0:T(4,128)S(1)} %pad_maximum_fusion.17) | data formatting | bytes 1048576 | tf_op jit(solution)/shard_map/stack | solution.py:37
  87.4 8.6 %gather_fusion = f32[1024,4]{1,0:T(8,128)S(1)} fusion(f32[4,32768]{0,1:T(8,128)} %copy.17, s32[1024]{0:T(1024)S(1)} %broadcast_clamp_fusion), kind=kCustom, calls=%fused_computation | custom fusion | bytes 36864 | tf_op jit(solution)/shard_map/jit(_take)/gather | solution.py:63
  96.1 0.6 select_bitcast_fusion
  96.7 3.3 %all-to-all-start = ((f32[8,4,128]{2,1,0:T(4,128)}), f32[8,4,128]{2,1,0:T(4,128)S(1)}, u32[]{:S(2)}, u32[]{:S(2)}) async-start(f32[8,4,128]{2,1,0:T(4,128)} %select_bitcast_fusion), calls=%async_computation | async-start | bytes 32768 | tf_op jit(solution)/shard_map/all_to_all | solution.py:67
  100.1 0.8 pad_maximum_fusion.16
  100.9 4.7 %all-to-all-done = f32[8,4,128]{2,1,0:T(4,128)S(1)} async-done(((f32[8,4,128]{2,1,0:T(4,128)}), f32[8,4,128]{2,1,0:T(4,128)S(1)}, u32[]{:S(2)}, u32[]{:S(2)}) %all-to-all-start) | async-done | bytes 16416 | tf_op jit(solution)/shard_map/all_to_all | solution.py:67
  105.6 0.6 fusion.27
  (28 shorter events, 1.6 us)
Async XLA Ops:
  7.2 33.7 %all-gather.2.cloned.1.call-start = ((), (), s32[]{:S(2)}) async-start(), calls=%async_computation.1 | async-start | bytes 1474560 | tf_op jit(solution)/shard_map/all_gather | solution.py:54
  10.4 32.0 %collective-permute-start.1 = (f32[1,4,16,16,1]{4,3,2,1,0:T(8,128)S(1)}, f32[1,4,16,16,1]{4,3,2,1,0:T(8,128)S(1)}, u32[]{:S(2)}, u32[]{:S(2)}) collective-permute-start(f32[1,4,16,16,1]{4,3,2,1,0:T(8,128)S(1)} %get-tuple-element.29), channel_id=1, source_target_pairs={{0,4},{4,8},{8,12},{12,16},{16,20},{20,24},{24,28},{28,0},{1,5},{5... | collective-permute-start | bytes 12296 | tf_op jit(solution)/shard_map/ppermute | solution.py:14
  10.9 31.5 %collective-permute-start = (f32[1,4,16,16,1]{4,3,2,1,0:T(8,128)S(1)}, f32[1,4,16,16,1]{4,3,2,1,0:T(8,128)S(1)}, u32[]{:S(2)}, u32[]{:S(2)}) collective-permute-start(f32[1,4,16,16,1]{4,3,2,1,0:T(8,128)S(1)} %get-tuple-element.30), channel_id=1, source_target_pairs={{4,0},{8,4},{12,8},{16,12},{20,16},{24,20},{28,24},{0,28},{5,1},{9... | collective-permute-start | bytes 12296 | tf_op jit(solution)/shard_map/ppermute | solution.py:15
  46.5 14.2 %collective-permute-start.3 = (f32[1,4,16,16,1]{4,3,2,1,0:T(8,128)S(1)}, f32[1,4,16,16,1]{4,3,2,1,0:T(8,128)S(1)}, u32[]{:S(2)}, u32[]{:S(2)}) collective-permute-start(f32[1,4,16,16,1]{4,3,2,1,0:T(8,128)S(1)} %get-tuple-element.27), channel_id=1, source_target_pairs={{0,4},{4,8},{8,12},{12,16},{16,20},{20,24},{24,28},{28,0},{1,5},{5... | collective-permute-start | bytes 12296 | tf_op jit(solution)/shard_map/ppermute | solution.py:14
  46.6 14.1 %collective-permute-start.2 = (f32[1,4,16,16,1]{4,3,2,1,0:T(8,128)S(1)}, f32[1,4,16,16,1]{4,3,2,1,0:T(8,128)S(1)}, u32[]{:S(2)}, u32[]{:S(2)}) collective-permute-start(f32[1,4,16,16,1]{4,3,2,1,0:T(8,128)S(1)} %get-tuple-element.28), channel_id=1, source_target_pairs={{4,0},{8,4},{12,8},{16,12},{20,16},{24,20},{28,24},{0,28},{5,1},{9... | collective-permute-start | bytes 12296 | tf_op jit(solution)/shard_map/ppermute | solution.py:15
  60.7 44.9 %copy-start = (f32[1,8,4,128]{3,2,1,0:T(4,128)S(1)}, f32[1,8,4,128]{3,2,1,0:T(4,128)}, u32[]{:S(2)}) copy-start(f32[1,8,4,128]{3,2,1,0:T(4,128)} %param.11) | copy-start | bytes 49156
  61.6 15.9 %collective-permute-start.5 = (f32[1,4,16,16,1]{4,3,2,1,0:T(8,128)S(1)}, f32[1,4,16,16,1]{4,3,2,1,0:T(8,128)S(1)}, u32[]{:S(2)}, u32[]{:S(2)}) collective-permute-start(f32[1,4,16,16,1]{4,3,2,1,0:T(8,128)S(1)} %get-tuple-element.25), channel_id=1, source_target_pairs={{0,4},{4,8},{8,12},{12,16},{16,20},{20,24},{24,28},{28,0},{1,5},{5... | collective-permute-start | bytes 12296 | tf_op jit(solution)/shard_map/ppermute | solution.py:14
  63.4 14.2 %collective-permute-start.4 = (f32[1,4,16,16,1]{4,3,2,1,0:T(8,128)S(1)}, f32[1,4,16,16,1]{4,3,2,1,0:T(8,128)S(1)}, u32[]{:S(2)}, u32[]{:S(2)}) collective-permute-start(f32[1,4,16,16,1]{4,3,2,1,0:T(8,128)S(1)} %get-tuple-element.26), channel_id=1, source_target_pairs={{4,0},{8,4},{12,8},{16,12},{20,16},{24,20},{28,24},{0,28},{5,1},{9... | collective-permute-start | bytes 12296 | tf_op jit(solution)/shard_map/ppermute | solution.py:15
  96.7 8.9 %all-to-all-start = ((f32[8,4,128]{2,1,0:T(4,128)}), f32[8,4,128]{2,1,0:T(4,128)S(1)}, u32[]{:S(2)}, u32[]{:S(2)}) async-start(f32[8,4,128]{2,1,0:T(4,128)} %select_bitcast_fusion), calls=%async_computation | async-start | bytes 32768 | tf_op jit(solution)/shard_map/all_to_all | solution.py:67
Sparse Core Ops, SparseCore 0:
  10.4 30.4 all-gather.1
where the time goes:
time: 113 us
  waiting for transfers between devices  52.1 us (46%)
  local copies, waits for them, and re-layouts  21.1 us (19%)
  starting transfers between devices  15.1 us (13%)
  between operations  14.2 us (13%)
  other arithmetic  10.6 us (9%)
    all_gather x1, waiting for transfers between devices, on_device(): gathered = lax.all_gather(trajectory, 'member', axis=1, tiled=True)  24.5 us
    ppermute x3, waiting for transfers between devices, with_halo(): before = lax.ppermute(last, axis, up)  22.9 us
    ppermute x3, starting transfers between devices, with_halo(): after = lax.ppermute(first, axis, down)  9.49 us
    gather x2, local copies, waits for them, and re-layouts, on_device(): picked = jnp.take(flat, index.reshape(-1), axis=1).reshape(4, tiles, slots)  8.76 us
    another operation x2, local copies, waits for them, and re-layouts, update(): return jnp.stack([fresh[:, 0], fresh[:, 1], temper, humid], axis=1)  8.71 us
    all_to_all x1, waiting for transfers between devices, on_device(): lax.all_to_all(outgoing, 'space', split_axis=0, concat_axis=0, tiled=True)  4.74 us
    add x3, other arithmetic, update(): fresh - across * (north - south) * 0.5  3.89 us
    all_to_all x1, starting transfers between devices, on_device(): lax.all_to_all(outgoing, 'space', split_axis=0, concat_axis=0, tiled=True)  3.31 us
  transfers between devices with their start and end apart: 8, of which 4 were waited for; matrix products, arithmetic and copies ran while one was open for 5% of the time, Pallas kernels for 0%

commit v1 on v0

v1 whole, which is shorter than its diff:
```python
import functools

import jax
import jax.numpy as jnp
from jax import lax
from jax.experimental import pallas as pl
from jax.experimental.pallas import tpu as pltpu
from jax.sharding import PartitionSpec as P

MESH = pl.DeviceIdType.MESH
F32 = jnp.float32
BF16 = jnp.bfloat16
FIELDS = 4


def kernel(
    members,
    tiles,
    pert,
    traj,
    scol,
    slev,
    counts,
    weights,
    final,
    equiv,
    state,
    coef,
    halo_out,
    halo_in,
    col_v,
    lev_v,
    w_own,
    w_in,
    key_v,
    onehot,
    table,
    picked,
    obs_out,
    obs_in,
    in_sem,
    fin_sem,
    own_send,
    own_recv,
    fwd_send,
    fwd_recv,
    halo_send,
    halo_recv,
    w_send,
    w_recv,
    obs_send,
    obs_recv,
):
    nsteps, per = traj.shape[0], traj.shape[1]
    levels, rows, lanes = pert.shape[2], pert.shape[3], pert.shape[4]
    slots = scol.shape[2]
    me = lax.axis_index("member")
    tile = lax.axis_index("space")
    square = members == 4 and per % 2 == 0

    if square:
        xn = me + 1 - 2 * lax.rem(me, 2)
        yn = lax.rem(me + 2, 4)
        sources = [me, xn, yn, 3 - me]
        direct = [xn, yn]
        senders = [xn, yn]
    else:
        sources = [lax.rem(me + members - j, members) for j in range(members)]
        senders = sources[1:]
        direct = [lax.rem(me + j, members) for j in range(1, members)]
    east = lax.rem(tile + 1, tiles)
    west = lax.rem(tile + tiles - 1, tiles)
    owners = [lax.rem(tile + j, tiles) for j in range(tiles)]

    load_state = pltpu.make_async_copy(pert.at[0], state, in_sem.at[0])
    load_own = [
        pltpu.make_async_copy(traj.at[k], coef.at[k, me], in_sem.at[4 + k])
        for k in range(nsteps)
    ]
    load_col = pltpu.make_async_copy(scol, col_v, in_sem.at[1])
    load_lev = pltpu.make_async_copy(slev, lev_v, in_sem.at[2])
    load_w = pltpu.make_async_copy(weights.at[0, tile], w_in.at[tile], in_sem.at[3])
    load_state.start()
    load_own[0].start()
    load_col.start()
    load_lev.start()
    load_w.start()
    for copy in load_own[1:]:
        copy.start()

    def send_own(k, j):
        return pltpu.make_async_remote_copy(
            src_ref=traj.at[k],
            dst_ref=coef.at[k, me],
            send_sem=own_send.at[k, j],
            recv_sem=own_recv.at[k, j],
            device_id={"member": direct[j]},
            device_id_type=MESH,
        )

    def forward(k, j):
        half = per // 2
        part = coef.at[k, senders[1 - j], pl.ds(j * half, half)]
        return pltpu.make_async_remote_copy(
            src_ref=part,
            dst_ref=part,
            send_sem=fwd_send.at[k, j],
            recv_sem=fwd_recv.at[k, j],
            device_id={"member": direct[j]},
            device_id_type=MESH,
        )

    def send_halo(k, side):
        return pltpu.make_async_remote_copy(
            src_ref=halo_out.at[k],
            dst_ref=halo_in.at[k, side],
            send_sem=halo_send.at[k, side],
            recv_sem=halo_recv.at[k, side],
            device_id={"space": (east, west)[side]},
            device_id_type=MESH,
        )

    def send_w(j):
        return pltpu.make_async_remote_copy(
            src_ref=weights.at[0, owners[j]],
            dst_ref=w_in.at[tile],
            send_sem=w_send.at[j],
            recv_sem=w_recv.at[j],
            device_id={"space": owners[j]},
            device_id_type=MESH,
        )

    def send_obs(j):
        return pltpu.make_async_remote_copy(
            src_ref=obs_out.at[owners[j]],
            dst_ref=obs_in.at[tile],
            send_sem=obs_send.at[j],
            recv_sem=obs_recv.at[j],
            device_id={"space": owners[j]},
            device_id_type=MESH,
        )

    ways = range(len(direct))

    barrier = pltpu.get_barrier_semaphore()
    for peer in direct:
        pl.semaphore_signal(barrier, inc=1, device_id={"member": peer}, device_id_type=MESH)
    for j in range(1, tiles):
        pl.semaphore_signal(barrier, inc=1, device_id={"space": owners[j]}, device_id_type=MESH)
    pl.semaphore_wait(barrier, len(direct) + tiles - 1)

    for k in range(min(2, nsteps)):
        for j in ways:
            send_own(k, j).start()

    lane = lax.broadcasted_iota(jnp.int32, (rows, lanes), 1)
    row = lax.broadcasted_iota(jnp.int32, (rows, lanes), 0)
    first, last = lane == 0, lane == lanes - 1
    edge = first | last
    even = lax.rem(lane, 2) == 0

    def pack(p, q):
        kept = jnp.where(edge, p, 0.0)
        return kept if q == 0 else pltpu.roll(kept, 2 * q, 1)

    load_state.wait()
    total = None
    for c, src in enumerate(sources):
        for l in range(per):
            for f in range(FIELDS):
                term = pack(state[f, src * per + l], f * levels + c * per + l)
                total = term if total is None else total + term
    halo_out[0] = total
    for side in range(2):
        send_halo(0, side).start()
    for j in range(1, tiles):
        send_w(j).start()

    load_col.wait()
    load_lev.wait()
    lat_iota = lax.broadcasted_iota(jnp.int32, (lanes, slots), 0)
    slot_iota = lax.broadcasted_iota(jnp.int32, (1, slots), 1)
    for o in range(tiles):
        col, lev = col_v[o], lev_v[o]
        lon = lax.rem(col, lanes)
        key = lev * rows + lax.div(col, lanes)
        key_v[o] = jnp.where(slot_iota < counts[o, 0], key, -1)
        hot = jnp.where(lat_iota == lon, 1.0, 0.0).astype(BF16)
        onehot[0:lanes, o * slots : (o + 1) * slots] = hot
        onehot[lanes : 2 * lanes, o * slots : (o + 1) * slots] = hot
    picked[...] = jnp.zeros_like(picked)

    def work(k, c, halo, total):
        src = sources[c]
        for l in range(per):
            at = src * per + l
            planes = [coef[k, src, l, i].astype(F32) for i in range(6)]
            a, b = planes[0], planes[1]
            ha, hb = 0.5 * a, 0.5 * b
            aa, bb = ha * a, hb * b
            to_e, to_w = aa - ha, aa + ha
            to_n = jnp.where(row == rows - 1, 0.0, bb - hb)
            to_s = jnp.where(row == 0, 0.0, bb + hb)
            stay = 1.0 - 2.0 * (aa + bb)
            old = [state[f, at] for f in range(FIELDS)]
            for f in range(FIELDS):
                p, q = old[f], f * levels + c * per + l
                side = halo if q == 0 else pltpu.roll(halo, lanes - 2 * q, 1)
                e = jnp.where(last, side, pltpu.roll(p, lanes - 1, 1))
                w = jnp.where(first, side, pltpu.roll(p, 1, 1))
                n = pltpu.roll(p, rows - 1, 0)
                s = pltpu.roll(p, 1, 0)
                new = stay * p + (to_e * e + to_w * w) + (to_n * n + to_s * s)
                if f == 2:
                    new = new - (planes[2] * old[0] + planes[3] * old[1])
                if f == 3:
                    new = new - (planes[4] * old[0] + planes[5] * old[1])
                state[f, at] = new
                if k < nsteps - 1:
                    term = pack(new, q)
                    total = term if total is None else total + term
                else:
                    high = new.astype(BF16)
                    low = (new - high.astype(F32)).astype(BF16)
                    base = (f * per + l) * rows
                    table[base : base + rows, 0:lanes] = high
                    table[base : base + rows, lanes : 2 * lanes] = low
        return total

    def finish(c):
        src = sources[c]
        save(c).start()
        for o in range(tiles):
            vals = jnp.dot(
                table[...],
                onehot[:, o * slots : (o + 1) * slots],
                preferred_element_type=F32,
            )
            key = key_v[o]
            lat = lax.broadcasted_iota(jnp.int32, (rows, slots), 0)
            acc = picked[o]
            for l in range(per):
                some = None
                for f in range(FIELDS):
                    base = (f * per + l) * rows
                    term = w_in[o, f : f + 1, :] * vals[base : base + rows]
                    some = term if some is None else some + term
                acc = acc + jnp.where(key == lat + (src * per + l) * rows, some, 0.0)
            picked[o] = acc

    def save(c):
        span = pl.ds(sources[c] * per, per)
        return pltpu.make_async_copy(
            state.at[:, span], final.at[0, :, span], fin_sem.at[c]
        )

    def arrived(k):
        for j in ways:
            send_own(k, j).wait_recv()
            if square:
                forward(k, 1 - j).start()

    arrived(0)
    for k in range(nsteps):
        if k + 2 < nsteps:
            for j in ways:
                send_own(k + 2, j).start()
        for side in range(2):
            send_halo(k, side).wait_recv()
        halo = jnp.where(
            even,
            pltpu.roll(halo_in[k, 0], 1, 1),
            pltpu.roll(halo_in[k, 1], lanes - 1, 1),
        )
        load_own[k].wait()
        if k == nsteps - 1:
            load_w.wait()
            for j in range(1, tiles):
                send_w(j).wait_recv()
        total = None
        for c in range(len(sources)):
            if square and c == 3:
                if k + 1 < nsteps:
                    arrived(k + 1)
                for j in ways:
                    forward(k, j).wait_recv()
            total = work(k, c, halo, total)
            if k == nsteps - 1:
                finish(c)
        if not square and k + 1 < nsteps:
            arrived(k + 1)
        if k + 1 < nsteps:
            halo_out[k + 1] = total
            for side in range(2):
                send_halo(k + 1, side).start()

    for o in range(tiles):
        obs_out[o] = jnp.sum(picked[o], axis=0, keepdims=True)
    for j in range(1, tiles):
        send_obs(j).start()
    obs_in[tile] = obs_out[tile]
    for k in range(nsteps):
        for j in ways:
            send_own(k, j).wait_send()
            if square:
                forward(k, j).wait_send()
        for side in range(2):
            send_halo(k, side).wait_send()
    for j in range(1, tiles):
        send_w(j).wait_send()
    for c in range(len(sources)):
        save(c).wait()
    for j in range(1, tiles):
        send_obs(j).wait_recv()
    for o in range(tiles):
        equiv[0, 0, o : o + 1, :] = obs_in[o]
    for j in range(1, tiles):
        send_obs(j).wait_send()


def on_device(perturbation, trajectory, site_col, site_lev, obs_counts, obs_weights):
    members = lax.axis_size("member")
    tiles = lax.axis_size("space")
    nsteps, per, planes, rows, lanes = trajectory.shape
    levels = perturbation.shape[2]
    slots = site_col.shape[2]
    any_space = pl.BlockSpec(memory_space=pl.ANY)
    dma = pltpu.SemaphoreType.DMA
    near = 2 if members == 4 and per % 2 == 0 else members - 1
    return pl.pallas_call(
        functools.partial(kernel, members, tiles),
        out_shape=(
            jax.ShapeDtypeStruct(perturbation.shape, F32),
            jax.ShapeDtypeStruct((1, 1, tiles, slots), F32),
        ),
        in_specs=[any_space] * 4 + [pl.BlockSpec(memory_space=pltpu.SMEM), any_space],
        out_specs=(any_space, pl.BlockSpec(memory_space=pltpu.VMEM)),
        scratch_shapes=[
            pltpu.VMEM((FIELDS, levels, rows, lanes), F32),
            pltpu.VMEM((nsteps, members, per, planes, rows, lanes), BF16),
            pltpu.VMEM((nsteps, rows, lanes), F32),
            pltpu.VMEM((nsteps, 2, rows, lanes), F32),
            pltpu.VMEM((tiles, 1, slots), jnp.int32),
            pltpu.VMEM((tiles, 1, slots), jnp.int32),
            pltpu.VMEM((FIELDS, slots), F32),
            pltpu.VMEM((tiles, FIELDS, slots), F32),
            pltpu.VMEM((tiles, 1, slots), jnp.int32),
            pltpu.VMEM((2 * lanes, tiles * slots), BF16),
            pltpu.VMEM((FIELDS * per * rows, 2 * lanes), BF16),
            pltpu.VMEM((tiles, rows, slots), F32),
            pltpu.VMEM((tiles, 1, slots), F32),
            pltpu.VMEM((tiles, 1, slots), F32),
            dma((4 + nsteps,)),
            dma((members,)),
            dma((nsteps, near)),
            dma((nsteps, near)),
            dma((nsteps, near)),
            dma((nsteps, near)),
            dma((nsteps, 2)),
            dma((nsteps, 2)),
            dma((tiles,)),
            dma((tiles,)),
            dma((tiles,)),
            dma((tiles,)),
        ],
        compiler_params=pltpu.CompilerParams(
            collective_id=0, has_side_effects=True, vmem_limit_bytes=32 * 1024 * 1024
        ),
        name="advect_observe",
    )(perturbation, trajectory, site_col, site_lev, obs_counts, obs_weights)


def solution(mesh):
    in_specs = (
        P("member", None, None, None, "space"),
        P(None, "member", None, None, "space"),
        P(None, "space", None),
        P(None, "space", None),
        P(None, "space"),
        P("space", None, None, None),
    )
    out_specs = (P("member", None, None, None, "space"), P("member", "space", None, None))
    return jax.shard_map(
        on_device, mesh=mesh, in_specs=in_specs, out_specs=out_specs, check_vma=False
    )
```

time: 113 us -> 35.2 us (0.31)
  waiting for transfers between devices: 52.1 us -> 0 us
  Pallas kernels: 0 us -> 28.7 us
  local copies, waits for them, and re-layouts: 21.1 us -> 5.53 us
  starting transfers between devices: 15.1 us -> 0 us
  between operations: 14.2 us -> 0.65 us
  other arithmetic: 10.6 us -> 0 us
    pallas_call x0 -> x1, Pallas kernels: none -> 28.7 us  [on_device(): pl.pallas_call(functools.partial(kernel, members, tiles), out_shape=(jax....]
    all_gather x1 -> x0, waiting for transfers between devices: 24.5 us -> none  [on_device(): gathered = lax.all_gather(trajectory, 'member', axis=1, tiled=True)]
    ppermute x6 -> x0, waiting for transfers between devices: 22.9 us -> none  [the longest x3 22.9 us: with_halo(): before = lax.ppermute(last, axis, up)]
    ppermute x6 -> x0, starting transfers between devices: 11.8 us -> none  [the longest x3 9.49 us: with_halo(): after = lax.ppermute(first, axis, down)]
    gather x2 -> x0, local copies, waits for them, and re-layouts: 8.76 us -> none  [on_device(): picked = jnp.take(flat, index.reshape(-1), axis=1).reshape(4, tiles, slots)]
    another operation x2 -> x0, local copies, waits for them, and re-layouts: 8.71 us -> none  [update(): return jnp.stack([fresh[:, 0], fresh[:, 1], temper, humid], axis=1)]
    all_to_all x1 -> x0, waiting for transfers between devices: 4.74 us -> none  [on_device(): lax.all_to_all(outgoing, 'space', split_axis=0, concat_axis=0, tiled=True)]
    add x3 -> x0, other arithmetic: 3.89 us -> none  [update(): fresh - across * (north - south) * 0.5]
  transfers between devices with their start and end apart: 8 -> 0, of which waited for: 4 -> 0; matrix products, arithmetic and copies ran while one was open for 5% -> 0% of each run, Pallas kernels for 0% -> 0%
where the time goes in v1:
time: 35.2 us; the launch traced here: 34.9 us
  Pallas kernels  28.7 us (82%)
  local copies, waits for them, and re-layouts  5.53 us (16%)
  between operations  0.65 us (2%)
    pallas_call x1, Pallas kernels, on_device(): pl.pallas_call(functools.partial(kernel, members, tiles), out_shape=(jax....  28.7 us
    unnamed x13, local copies, waits for them, and re-layouts  5.53 us

profile of v1, /device:TPU:0, one launch (start us, length us, event | category | flops | bytes accessed | tf_op | source)
XLA Modules:
  0.0 34.9 jit_solution(13302562738289105889)
XLA Ops:
  0.6 0.0 copy-start.3
  0.6 0.7 %copy.8.counts = s32[8,1]{1,0:T(8,128)S(1)} copy(s32[8,1]{0,1:T(1,128)} %param.10) | data formatting | bytes 64 | tf_op args[4]
  1.4 0.0 copy-done.3
  1.4 0.0 copy-start
  1.4 1.0 %copy-done = f32[1,4,16,16,128]{4,3,2,1,0:T(8,128)S(1)} copy-done((f32[1,4,16,16,128]{4,3,2,1,0:T(8,128)S(1)}, f32[1,4,16,16,128]{4,3,2,1,0:T(8,128)}, u32[]{:S(2)}) %copy-start) | copy-done | bytes 524312
  2.4 0.0 copy-start.1
  2.4 1.0 %copy-done.1 = bf16[3,4,6,16,128]{4,3,2,1,0:T(8,128)(2,1)S(1)} copy-done((bf16[3,4,6,16,128]{4,3,2,1,0:T(8,128)(2,1)S(1)}, bf16[3,4,6,16,128]{4,3,2,1,0:T(8,128)(2,1)}, u32[]{:S(2)}) %copy-start.1) | copy-done | bytes 294936
  3.4 0.0 copy-start.2
  3.4 0.7 %copy-done.2 = f32[1,8,4,128]{3,2,1,0:T(4,128)S(1)} copy-done((f32[1,8,4,128]{3,2,1,0:T(4,128)S(1)}, f32[1,8,4,128]{3,2,1,0:T(4,128)}, u32[]{:S(2)}) %copy-start.2) | copy-done | bytes 16408
  4.1 0.0 copy-start.4
  4.1 0.7 %copy-done.4 = s32[8,1,128]{2,1,0:T(1,128)S(1)} copy-done((s32[8,1,128]{2,1,0:T(1,128)S(1)}, s32[8,1,128]{2,1,0:T(1,128)}, u32[]{:S(2)}) %copy-start.4) | copy-done | bytes 4120
  4.8 28.7 %advect_observe.1 = (f32[1,4,16,16,128]{4,3,2,1,0:T(8,128)S(1)}, f32[1,1,8,128]{3,2,1,0:T(8,128)S(1)}) custom-call(f32[1,4,16,16,128]{4,3,2,1,0:T(8,128)S(1)} %copy-done, bf16[3,4,6,16,128]{4,3,2,1,0:T(8,128)(2,1)S(1)} %copy-done.1, s32[8,1,128]{2,1,0:T(1,128)S(1)} %copy-done.3, s32[8,1,128]{2,1,0:T(1,128)S(1)} %copy-done.4, s32[8,1]{1,0:T(8,128)S(1)} %copy.8.counts, ...), custom_call_target="tpu_custom_call" | custom-call | tf_op jit(solution)/shard_map/advect_observe/pallas_call | solution.py:330
  33.5 0.8 %copy.11 = f32[1,4,16,16,128]{4,3,2,1,0:T(8,128)} copy(f32[1,4,16,16,128]{4,3,2,1,0:T(8,128)S(1)} %get-tuple-element.4) | data formatting | bytes 1048576
  34.3 0.6 %copy.12 = f32[1,1,8,128]{3,2,1,0:T(8,128)} copy(f32[1,1,8,128]{3,2,1,0:T(8,128)S(1)} %get-tuple-element.5) | data formatting | bytes 8192
Async XLA Ops:
  0.6 0.7 %copy-start.3 = (s32[8,1,128]{2,1,0:T(1,128)S(1)}, s32[8,1,128]{2,1,0:T(1,128)}, u32[]{:S(2)}) copy-start(s32[8,1,128]{2,1,0:T(1,128)} %scol.1) | copy-start | bytes 12292
  1.4 1.0 %copy-start = (f32[1,4,16,16,128]{4,3,2,1,0:T(8,128)S(1)}, f32[1,4,16,16,128]{4,3,2,1,0:T(8,128)}, u32[]{:S(2)}) copy-start(f32[1,4,16,16,128]{4,3,2,1,0:T(8,128)} %pert.1) | copy-start | bytes 1572868
  2.4 1.0 %copy-start.1 = (bf16[3,4,6,16,128]{4,3,2,1,0:T(8,128)(2,1)S(1)}, bf16[3,4,6,16,128]{4,3,2,1,0:T(8,128)(2,1)}, u32[]{:S(2)}) copy-start(bf16[3,4,6,16,128]{4,3,2,1,0:T(8,128)(2,1)} %traj.1) | copy-start | bytes 884740
  3.4 0.7 %copy-start.2 = (f32[1,8,4,128]{3,2,1,0:T(4,128)S(1)}, f32[1,8,4,128]{3,2,1,0:T(4,128)}, u32[]{:S(2)}) copy-start(f32[1,8,4,128]{3,2,1,0:T(4,128)} %weights.1) | copy-start | bytes 49156
  4.1 0.7 %copy-start.4 = (s32[8,1,128]{2,1,0:T(1,128)S(1)}, s32[8,1,128]{2,1,0:T(1,128)}, u32[]{:S(2)}) copy-start(s32[8,1,128]{2,1,0:T(1,128)} %slev.1) | copy-start | bytes 12292
